TPU v7x, 256 devices: a whole 4x4x8 slice. The times are simulated.
256 devices in a mesh: dp: 16 (over z_lo, x), context: 16 (over z_hi, y, core).
Axes of the slice: x: 4, y: 4, z: 8 (z_hi: 2, z_lo: 4; z = z_hi * 4 + z_lo), core: 2. Of those that a mesh axis runs over, the one named last changes fastest.
Arguments:
- queries: bfloat16 [16, 2048, 4096], P('dp', 'context'), may hold values from -8 to 8
- keys_values: bfloat16 [16, 2048, 2, 512], P('dp', 'context'), may hold values from -8 to 8
- key_tangents: bfloat16 [16, 2048, 2, 512], P('dp', 'context'), may hold values from -20 to 20
- output_adjoint_rows: bfloat16 [16, 2048, 4096], P('dp', 'context'), may hold values from -0.59765625 to 0.59765625
- segments: int32 [16, 2048], P('dp'), may hold values from 0 to 3, as said below
- span_pair: int32 [16], replicated, may hold values from 0 to 15, as said below
Outputs:
- hess_queries: bfloat16 [16, 2048, 4096], P('dp', 'context')
- hess_keys_values: bfloat16 [16, 2048, 2, 512], P('dp', 'context')
- curvature: float32 [], replicated
Inputs may be any that keep to these rules, and one draw needn't show every extreme that they name: `span_pair`: A permutation of 0 to 15. `segments`: ids never fall along positions within a window, start at 0, and every window holds exactly four documents.
All inputs are finite; a program needn't handle non-finite values.
Results may differ from a plain program's by a relative error of at most 0.03.
Values may be sent and summed in bfloat16 or wider, within the bound.
A program may use at most 256 MiB of HBM per device.

v0:
```python
import math

import jax
import jax.numpy as jnp
from jax import lax
from jax.sharding import PartitionSpec as P

HEAD_SIZE = 128
QUERY_HEADS = 32
KEY_VALUE_HEADS = 4


def positions(rows, pair, tok_dev):
    span = tok_dev // 2
    token_count = pair.shape[0]
    device = rows // tok_dev
    within = rows % tok_dev
    table = jnp.arange(token_count, dtype=jnp.int32)
    first = jnp.sum(jnp.where(device[:, None] == table[None, :], pair[None, :], 0), axis=1)
    block = jnp.where(within // span == 0, first, 2 * token_count - 1 - first)
    return block * span + within % span


def on_device(queries, keys_values, key_tangents, output_adjoint_rows, segments, span_pair):
    token_index = queries.shape[1]
    shards = lax.axis_size("context")
    span_length = token_index * shards
    query_group = QUERY_HEADS // KEY_VALUE_HEADS
    scale = float(HEAD_SIZE) ** (-0.5)
    here = lax.axis_index("context")
    own_rows = here * token_index + jnp.arange(token_index, dtype=jnp.int32)
    own_pos = positions(own_rows, span_pair, token_index)
    own_seg = lax.dynamic_slice_in_dim(segments[0], here * token_index, token_index)
    query_head_rows = queries[0].reshape(token_index, KEY_VALUE_HEADS, query_group, HEAD_SIZE)
    output_adjoint = output_adjoint_rows[0].reshape(
        token_index, KEY_VALUE_HEADS, query_group, HEAD_SIZE
    )

    def unpack(pieces, start):
        value_portion, tangent_portion = pieces
        token_count = value_portion.shape[1]
        key_matrix = value_portion[0, :, 0].reshape(token_count, KEY_VALUE_HEADS, HEAD_SIZE)
        value_matrix = value_portion[0, :, 1].reshape(token_count, KEY_VALUE_HEADS, HEAD_SIZE)
        key_direction = tangent_portion[0, :, 0].reshape(token_count, KEY_VALUE_HEADS, HEAD_SIZE)
        value_direction = tangent_portion[0, :, 1].reshape(token_count, KEY_VALUE_HEADS, HEAD_SIZE)
        key_rows = start + jnp.arange(token_count, dtype=jnp.int32)
        key_pos = positions(key_rows, span_pair, token_index)
        key_seg = lax.dynamic_slice_in_dim(segments[0], start, token_count)
        seen = (key_pos[None, :] <= own_pos[:, None]) & (key_seg[None, :] == own_seg[:, None])
        return (seen, key_matrix, value_matrix, key_direction, value_direction)

    def products(key_matrix, value_matrix, key_direction, value_direction):
        logits = scale * jnp.einsum(
            "thgd,shd->hgts", query_head_rows, key_matrix, preferred_element_type=jnp.float32
        )
        dprob = jnp.einsum(
            "thgd,shd->hgts", output_adjoint, value_matrix, preferred_element_type=jnp.float32
        )
        tlogits = scale * jnp.einsum(
            "thgd,shd->hgts", query_head_rows, key_direction, preferred_element_type=jnp.float32
        )
        tdprob = jnp.einsum(
            "thgd,shd->hgts", output_adjoint, value_direction, preferred_element_type=jnp.float32
        )
        return (logits, dprob, tlogits, tdprob)

    def stats_step(carry, pieces, start):
        seen, key_matrix, value_matrix, key_direction, value_direction = unpack(pieces, start)

        def stats_live(state):
            run_max, total, acc_mu, acc_delta, acc_extra, acc_tail = state
            logits, dprob, tlogits, tdprob = products(
                key_matrix, value_matrix, key_direction, value_direction
            )
            masked = jnp.where(seen, logits, jnp.float32(-1e30))
            new_max = jnp.maximum(run_max, jnp.max(masked, axis=-1, keepdims=True))
            decay = jnp.exp(run_max - new_max)
            weight = jnp.where(seen, jnp.exp(masked - new_max), jnp.float32(0.0))
            return (
                new_max,
                total * decay + jnp.sum(weight, axis=-1, keepdims=True),
                acc_mu * decay + jnp.sum(weight * tlogits, axis=-1, keepdims=True),
                acc_delta * decay + jnp.sum(weight * dprob, axis=-1, keepdims=True),
                acc_extra * decay + jnp.sum(weight * tlogits * dprob, axis=-1, keepdims=True),
                acc_tail * decay + jnp.sum(weight * tdprob, axis=-1, keepdims=True),
            )

        return lax.cond(jnp.any(seen), stats_live, lambda state: state, carry)

    empty_statistic = jnp.zeros((KEY_VALUE_HEADS, query_group, token_index, 1), jnp.float32)
    stat_init = (
        jnp.full((KEY_VALUE_HEADS, query_group, token_index, 1), -1e30, jnp.float32),
        empty_statistic,
        empty_statistic,
        empty_statistic,
        empty_statistic,
        empty_statistic,
    )

    def finish(stats):
        run_max, total, acc_mu, acc_delta, acc_extra, acc_tail = stats
        return (
            run_max,
            total,
            acc_mu / total,
            acc_delta / total,
            acc_extra / total,
            acc_tail / total,
        )

    def make_grads_step(stats):
        run_max, total, mean_t, delta, extra, tail = finish(stats)

        def grads_step(carry, pieces, start):
            seen, key_matrix, value_matrix, key_direction, value_direction = unpack(pieces, start)
            token_count = key_matrix.shape[0]

            def grads_live(state):
                query_acc, key_acc = state
                logits, dprob, tlogits, tdprob = products(
                    key_matrix, value_matrix, key_direction, value_direction
                )
                masked = jnp.where(seen, logits, jnp.float32(-1e30))
                prob = jnp.where(seen, jnp.exp(masked - run_max), jnp.float32(0.0)) / total
                tprob = prob * (tlogits - mean_t)
                dscore = prob * (dprob - delta)
                tdelta = extra - mean_t * delta + tail
                tdscore = tprob * (dprob - delta) + prob * (tdprob - tdelta)
                dscore_b = dscore.astype(jnp.bfloat16)
                tdscore_b = tdscore.astype(jnp.bfloat16)
                tprob_b = tprob.astype(jnp.bfloat16)
                query_term = jnp.einsum(
                    "hgts,shd->thgd", tdscore_b, key_matrix, preferred_element_type=jnp.float32
                )
                query_term = query_term + jnp.einsum(
                    "hgts,shd->thgd", dscore_b, key_direction, preferred_element_type=jnp.float32
                )
                key_gradient = scale * jnp.einsum(
                    "hgts,thgd->shd", tdscore_b, query_head_rows, preferred_element_type=jnp.float32
                )
                value_gradient = jnp.einsum(
                    "hgts,thgd->shd", tprob_b, output_adjoint, preferred_element_type=jnp.float32
                )
                block = jnp.stack(
                    [
                        key_gradient.reshape(token_count, KEY_VALUE_HEADS * HEAD_SIZE),
                        value_gradient.reshape(token_count, KEY_VALUE_HEADS * HEAD_SIZE),
                    ],
                    axis=1,
                )
                old = lax.dynamic_slice_in_dim(key_acc, start, token_count, 0)
                key_acc = lax.dynamic_update_slice_in_dim(key_acc, old + block, start, 0)
                return (query_acc + scale * query_term, key_acc)

            return lax.cond(jnp.any(seen), grads_live, lambda state: state, carry)

        return grads_step

    grad_init = (
        jnp.zeros((token_index, KEY_VALUE_HEADS, query_group, HEAD_SIZE), jnp.float32),
        jnp.zeros((span_length, 2, KEY_VALUE_HEADS * HEAD_SIZE), jnp.float32),
    )
    gathered = (
        lax.all_gather(keys_values, "context", axis=1, tiled=True),
        lax.all_gather(key_tangents, "context", axis=1, tiled=True),
    )
    per_step = token_index * math.gcd(shards, max(1, 512 // token_index))
    turns = span_length // per_step

    def sweep(step_fn, init):

        def turn(index, carry):
            start = jnp.asarray(index, jnp.int32) * per_step
            pieces = (
                lax.dynamic_slice_in_dim(gathered[0], start, per_step, 1),
                lax.dynamic_slice_in_dim(gathered[1], start, per_step, 1),
            )
            return step_fn(carry, pieces, start)

        return lax.fori_loop(0, turns, turn, init)

    stats = sweep(stats_step, stat_init)
    query_acc, key_acc = sweep(make_grads_step(stats), grad_init)
    key_hessian = lax.psum_scatter(key_acc, "context", scatter_dimension=0, tiled=True)
    local_term = jnp.sum(key_tangents[0].astype(jnp.float32) * key_hessian)
    total_term = lax.psum(local_term, ("dp", "context"))
    curvature = total_term / (lax.axis_size("dp") * span_length)
    hess_queries = query_acc.reshape(1, token_index, QUERY_HEADS * HEAD_SIZE).astype(jnp.bfloat16)
    return (hess_queries, key_hessian[None].astype(jnp.bfloat16), curvature)


def solution(mesh):
    in_specs = (
        P("dp", "context", None),
        P("dp", "context", None, None),
        P("dp", "context", None, None),
        P("dp", "context", None),
        P("dp", None),
        P(),
    )
    out_specs = (P("dp", "context", None), P("dp", "context", None, None), P())
    return jax.shard_map(
        on_device, mesh=mesh, in_specs=in_specs, out_specs=out_specs, check_vma=False
    )
```

profile of v0, /device:TPU:32, one launch (start us, length us, event | category | flops | bytes accessed | tf_op | source)
XLA Modules:
  0.0 764.6 jit_solution(3982877391161199131)
XLA Ops:
  18.1 73.1 %all-gather.3.cloned.1.call-done = bf16[1,2048,2,512]{1,3,2,0:T(8,128)(2,1)} async-done(((bf16[1,128,2,512]{1,3,2,0:T(8,128)(2,1)}), bf16[1,2048,2,512]{1,3,2,0:T(8,128)(2,1)}) %all-gather.3.cloned.1.call-update) | async-done | bytes 4194320 | tf_op jit(solution)/shard_map/all_gather | solution.py:164
  91.1 76.8 %all-gather.5.cloned.1.call-done = bf16[1,2048,2,512]{1,3,2,0:T(8,128)(2,1)} async-done(((bf16[1,128,2,512]{1,3,2,0:T(8,128)(2,1)}), bf16[1,2048,2,512]{1,3,2,0:T(8,128)(2,1)}) %all-gather.5.cloned.1.call-update) | async-done | bytes 4194320 | tf_op jit(solution)/shard_map/all_gather | solution.py:165
  168.0 60.2 %while.44 = (s32[]{:T(128)}, f32[4,8,128,1]{2,1,0,3:T(8,128)S(1)}, f32[4,8,128,1]{2,1,0,3:T(8,128)S(1)}, f32[4,8,128,1]{2,1,0,3:T(8,128)S(1)}, f32[4,8,128,1]{2,...) while((s32[]{:T(128)}, f32[4,8,128,1]{2,1,0,3:T(8,128)S(1)}, ...), condition=%wide.region_12.13_spmd, body=%wide.region_1.12_spmd.sunk | while | flops 2200249856 | bytes 65900068 | solution.py:180
  169.8 13.3 %conditional.4 = ((f32[4,8,128,1]{2,1,0,3:T(8,128)S(1)}, f32[4,8,128,1]{2,1,0,3:T(8,128)S(1)}, f32[4,8,128,1]{2,1,0,3:T(8,128)S(1)}, f32[4,8,128,1]{2,1,0,3:T(8,...) conditional(s32[]{:T(128)} %convert_element_type.80, (f32[4,8,128,1]{2,1,0,3:T(8,128)S(1)}, ...), branch_computations={%region_4.4_spmd, %region_5.11_spmd} | conditional | flops 2199937024 | bytes 65814632 | solution.py:88
  184.8 13.3 %conditional.4 = ((f32[4,8,128,1]{2,1,0,3:T(8,128)S(1)}, f32[4,8,128,1]{2,1,0,3:T(8,128)S(1)}, f32[4,8,128,1]{2,1,0,3:T(8,128)S(1)}, f32[4,8,128,1]{2,1,0,3:T(8,...) conditional(s32[]{:T(128)} %convert_element_type.80, (f32[4,8,128,1]{2,1,0,3:T(8,128)S(1)}, ...), branch_computations={%region_4.4_spmd, %region_5.11_spmd} | conditional | flops 2199937024 | bytes 65814632 | solution.py:88
  199.9 13.3 %conditional.4 = ((f32[4,8,128,1]{2,1,0,3:T(8,128)S(1)}, f32[4,8,128,1]{2,1,0,3:T(8,128)S(1)}, f32[4,8,128,1]{2,1,0,3:T(8,128)S(1)}, f32[4,8,128,1]{2,1,0,3:T(8,...) conditional(s32[]{:T(128)} %convert_element_type.80, (f32[4,8,128,1]{2,1,0,3:T(8,128)S(1)}, ...), branch_computations={%region_4.4_spmd, %region_5.11_spmd} | conditional | flops 2199937024 | bytes 65814632 | solution.py:88
  214.9 13.3 %conditional.4 = ((f32[4,8,128,1]{2,1,0,3:T(8,128)S(1)}, f32[4,8,128,1]{2,1,0,3:T(8,128)S(1)}, f32[4,8,128,1]{2,1,0,3:T(8,128)S(1)}, f32[4,8,128,1]{2,1,0,3:T(8,...) conditional(s32[]{:T(128)} %convert_element_type.80, (f32[4,8,128,1]{2,1,0,3:T(8,128)S(1)}, ...), branch_computations={%region_4.4_spmd, %region_5.11_spmd} | conditional | flops 2199937024 | bytes 65814632 | solution.py:88
  234.0 197.5 %while.45 = (s32[]{:T(128)}, f32[128,4,8,128]{3,0,2,1:T(8,128)}, f32[2048,2,512]{0,2,1:T(8,128)}, s32[16]{0:T(128)S(1)}, s32[128]{0:T(128)S(1)}, /*index=5*/s32[...) while((s32[]{:T(128)}, f32[128,4,8,128]{3,0,2,1:T(8,128)}, ...), condition=%wide.region_18.19_spmd, body=%wide.region_13.18_spmd.sunk | while | flops 4342216192 | bytes 181751440 | solution.py:180
  235.6 47.8 %conditional.5 = ((f32[128,4,8,128]{3,0,2,1:T(8,128)}, f32[2048,2,512]{0,2,1:T(8,128)})) conditional(s32[]{:T(128)} %convert_element_type.81, (f32[128,4,8,128]{3,0,2,1:T(8,128)}, f32[2048,2,512]{0,2,1:T(8,128)}) %tuple.136, (pred[128,512]{0,1:T(8,128)(4,1)S(1)}, bf16[1,2048,2,512]{1,3,2,0:T(8,128)(2,1)}, s32[]{:T(128)}, ...), branch_computations={%region_16.16_spmd, %region_17.17_spmd} | conditional | flops 4341903360 | bytes 181665984 | solution.py:155
  244.4 8.4 %fusion.22 = f32[4,512,128,1]{1,2,3,0:T(8,128)S(1)} fusion(bf16[128,4,8,128]{0,3,2,1:T(8,128)(2,1)} %get-tuple-element.1133, f32[4,8,128,512]{2,3,1,0:T(8,128)} %fusion.20, f32[4,512,128,8]{2,1,3,0:T(8,128)S(1)} %fusion.45, f32[4,8,128]{2,1,0:T(8,128)S(1)} %bitcast.194), kind=kOutput, calls=%fused_computation.62 | convolution fusion | flops 545259520 | bytes 18890752 | tf_op jit(solution)/shard_map/while/body/eval_jaxpr/cond/branch_1_fun/hgts,thgd->shd/dot_general | solution.py:141
  255.6 9.2 %fusion.15 = bf16[4,8,128,512]{2,3,1,0:T(8,128)(2,1)} fusion(f32[4,8,128,512]{2,3,1,0:T(8,128)} %fusion.20, f32[4,512,128,8]{2,1,3,0:T(8,128)S(1)} %fusion.46, f32[4,512,128,8]{2,1,3,0:T(8,128)} %copy-done, f32[4,8,128]{2,1,0:T(8,128)S(1)} %add_bitcast_fusion, f32[4,8,128]{2,1,0:T(8,128)S(1)} %bitcast.192, f32[4,8,128]{2,1,0:T(8,128)S(1)} %bitcast.195, ...), kind=kOutput, calls=%fused_computation.51 | convolution fusion | flops 555745280 | bytes 30982144 | tf_op jit(solution)/shard_map/while/body/eval_jaxpr/cond/branch_1_fun/thgd,shd->hgts/dot_general | solution.py:62
  264.8 7.0 fusion.24
  271.9 6.6 bitcast_add_fusion.5
  285.0 47.8 %conditional.5 = ((f32[128,4,8,128]{3,0,2,1:T(8,128)}, f32[2048,2,512]{0,2,1:T(8,128)})) conditional(s32[]{:T(128)} %convert_element_type.81, (f32[128,4,8,128]{3,0,2,1:T(8,128)}, f32[2048,2,512]{0,2,1:T(8,128)}) %tuple.136, (pred[128,512]{0,1:T(8,128)(4,1)S(1)}, bf16[1,2048,2,512]{1,3,2,0:T(8,128)(2,1)}, s32[]{:T(128)}, ...), branch_computations={%region_16.16_spmd, %region_17.17_spmd} | conditional | flops 4341903360 | bytes 181665984 | solution.py:155
  287.8 4.7 fusion.20
  293.8 8.4 %fusion.22 = f32[4,512,128,1]{1,2,3,0:T(8,128)S(1)} fusion(bf16[128,4,8,128]{0,3,2,1:T(8,128)(2,1)} %get-tuple-element.1133, f32[4,8,128,512]{2,3,1,0:T(8,128)} %fusion.20, f32[4,512,128,8]{2,1,3,0:T(8,128)S(1)} %fusion.45, f32[4,8,128]{2,1,0:T(8,128)S(1)} %bitcast.194), kind=kOutput, calls=%fused_computation.62 | convolution fusion | flops 545259520 | bytes 18890752 | tf_op jit(solution)/shard_map/while/body/eval_jaxpr/cond/branch_1_fun/hgts,thgd->shd/dot_general | solution.py:141
  305.0 9.2 %fusion.15 = bf16[4,8,128,512]{2,3,1,0:T(8,128)(2,1)} fusion(f32[4,8,128,512]{2,3,1,0:T(8,128)} %fusion.20, f32[4,512,128,8]{2,1,3,0:T(8,128)S(1)} %fusion.46, f32[4,512,128,8]{2,1,3,0:T(8,128)} %copy-done, f32[4,8,128]{2,1,0:T(8,128)S(1)} %add_bitcast_fusion, f32[4,8,128]{2,1,0:T(8,128)S(1)} %bitcast.192, f32[4,8,128]{2,1,0:T(8,128)S(1)} %bitcast.195, ...), kind=kOutput, calls=%fused_computation.51 | convolution fusion | flops 555745280 | bytes 30982144 | tf_op jit(solution)/shard_map/while/body/eval_jaxpr/cond/branch_1_fun/thgd,shd->hgts/dot_general | solution.py:62
  314.2 7.0 fusion.24
  321.3 6.6 bitcast_add_fusion.5
  334.4 47.8 %conditional.5 = ((f32[128,4,8,128]{3,0,2,1:T(8,128)}, f32[2048,2,512]{0,2,1:T(8,128)})) conditional(s32[]{:T(128)} %convert_element_type.81, (f32[128,4,8,128]{3,0,2,1:T(8,128)}, f32[2048,2,512]{0,2,1:T(8,128)}) %tuple.136, (pred[128,512]{0,1:T(8,128)(4,1)S(1)}, bf16[1,2048,2,512]{1,3,2,0:T(8,128)(2,1)}, s32[]{:T(128)}, ...), branch_computations={%region_16.16_spmd, %region_17.17_spmd} | conditional | flops 4341903360 | bytes 181665984 | solution.py:155
  343.2 8.4 %fusion.22 = f32[4,512,128,1]{1,2,3,0:T(8,128)S(1)} fusion(bf16[128,4,8,128]{0,3,2,1:T(8,128)(2,1)} %get-tuple-element.1133, f32[4,8,128,512]{2,3,1,0:T(8,128)} %fusion.20, f32[4,512,128,8]{2,1,3,0:T(8,128)S(1)} %fusion.45, f32[4,8,128]{2,1,0:T(8,128)S(1)} %bitcast.194), kind=kOutput, calls=%fused_computation.62 | convolution fusion | flops 545259520 | bytes 18890752 | tf_op jit(solution)/shard_map/while/body/eval_jaxpr/cond/branch_1_fun/hgts,thgd->shd/dot_general | solution.py:141
  354.4 9.2 %fusion.15 = bf16[4,8,128,512]{2,3,1,0:T(8,128)(2,1)} fusion(f32[4,8,128,512]{2,3,1,0:T(8,128)} %fusion.20, f32[4,512,128,8]{2,1,3,0:T(8,128)S(1)} %fusion.46, f32[4,512,128,8]{2,1,3,0:T(8,128)} %copy-done, f32[4,8,128]{2,1,0:T(8,128)S(1)} %add_bitcast_fusion, f32[4,8,128]{2,1,0:T(8,128)S(1)} %bitcast.192, f32[4,8,128]{2,1,0:T(8,128)S(1)} %bitcast.195, ...), kind=kOutput, calls=%fused_computation.51 | convolution fusion | flops 555745280 | bytes 30982144 | tf_op jit(solution)/shard_map/while/body/eval_jaxpr/cond/branch_1_fun/thgd,shd->hgts/dot_general | solution.py:62
  363.6 7.0 fusion.24
  370.7 6.6 bitcast_add_fusion.5
  383.8 47.7 %conditional.5 = ((f32[128,4,8,128]{3,0,2,1:T(8,128)}, f32[2048,2,512]{0,2,1:T(8,128)})) conditional(s32[]{:T(128)} %convert_element_type.81, (f32[128,4,8,128]{3,0,2,1:T(8,128)}, f32[2048,2,512]{0,2,1:T(8,128)}) %tuple.136, (pred[128,512]{0,1:T(8,128)(4,1)S(1)}, bf16[1,2048,2,512]{1,3,2,0:T(8,128)(2,1)}, s32[]{:T(128)}, ...), branch_computations={%region_16.16_spmd, %region_17.17_spmd} | conditional | flops 4341903360 | bytes 181665984 | solution.py:155
  392.5 8.4 %fusion.22 = f32[4,512,128,1]{1,2,3,0:T(8,128)S(1)} fusion(bf16[128,4,8,128]{0,3,2,1:T(8,128)(2,1)} %get-tuple-element.1133, f32[4,8,128,512]{2,3,1,0:T(8,128)} %fusion.20, f32[4,512,128,8]{2,1,3,0:T(8,128)S(1)} %fusion.45, f32[4,8,128]{2,1,0:T(8,128)S(1)} %bitcast.194), kind=kOutput, calls=%fused_computation.62 | convolution fusion | flops 545259520 | bytes 18890752 | tf_op jit(solution)/shard_map/while/body/eval_jaxpr/cond/branch_1_fun/hgts,thgd->shd/dot_general | solution.py:141
  403.7 9.2 %fusion.15 = bf16[4,8,128,512]{2,3,1,0:T(8,128)(2,1)} fusion(f32[4,8,128,512]{2,3,1,0:T(8,128)} %fusion.20, f32[4,512,128,8]{2,1,3,0:T(8,128)S(1)} %fusion.46, f32[4,512,128,8]{2,1,3,0:T(8,128)} %copy-done, f32[4,8,128]{2,1,0:T(8,128)S(1)} %add_bitcast_fusion, f32[4,8,128]{2,1,0:T(8,128)S(1)} %bitcast.192, f32[4,8,128]{2,1,0:T(8,128)S(1)} %bitcast.195, ...), kind=kOutput, calls=%fused_computation.51 | convolution fusion | flops 555745280 | bytes 30982144 | tf_op jit(solution)/shard_map/while/body/eval_jaxpr/cond/branch_1_fun/thgd,shd->hgts/dot_general | solution.py:62
  413.0 7.0 fusion.24
  420.0 6.6 bitcast_add_fusion.5
  431.5 13.2 %copy.100 = f32[2048,2,512]{2,1,0:T(2,128)} copy(f32[2048,2,512]{0,2,1:T(8,128)} %get-tuple-element.1177) | data formatting | bytes 16777216 | tf_op jit(solution)/shard_map/while | solution.py:180
  449.0 221.4 %all-reduce.3.cloned.1.call-done = f32[2048,2,512]{2,1,0:T(2,128)} async-done(((f32[2048,2,512]{2,1,0:T(2,128)}), f32[2048,2,512]{2,1,0:T(2,128)}) %all-reduce.3.cloned.1.call-update) | async-done | bytes 8388624
  673.9 80.5 %psum.7 = f32[]{:T(128)} all-reduce(f32[]{:T(128)} %fusion.39), channel_id=1, replica_groups=mesh['dp'=16,'context'=16] {'dp','context'}, use_global_device_ids=true, to_apply=%region_21.22 | all-reduce | flops 1 | bytes 8 | tf_op jit(solution)/shard_map/psum | solution.py:186
  (182 shorter events, 147.3 us)
Async XLA Ops:
  7.2 10.7 %copy-start.7 = (s32[1,2048]{1,0:T(1,128)S(1)}, s32[1,2048]{1,0:T(1,128)}, u32[]{:S(2)}) copy-start(s32[1,2048]{1,0:T(1,128)} %param.18) | copy-start | bytes 24580
  7.2 10.8 %copy-start.6 = (s32[16]{0:T(128)S(1)}, s32[16]{0:T(128)}, u32[]{:S(2)}) copy-start(s32[16]{0:T(128)} %param.19) | copy-start | bytes 196
  7.2 83.9 %all-gather.3.cloned.1.call-start = ((), (), s32[]{:S(2)}) async-start(), calls=%async_computation | async-start | bytes 4456448 | tf_op jit(solution)/shard_map/all_gather | solution.py:164
  9.1 158.9 %all-gather.5.cloned.1.call-start = ((), (), s32[]{:S(2)}) async-start(), calls=%async_computation.1 | async-start | bytes 4456448 | tf_op jit(solution)/shard_map/all_gather | solution.py:165
  11.0 659.4 %all-reduce.3.cloned.1.call-start = ((), (), s32[]{:S(2)}) async-start(), calls=%async_computation.2 | async-start | bytes 16777216
  171.4 1.5 copy-start.4
  186.5 1.5 copy-start.4
  201.6 1.5 copy-start.4
  216.6 1.5 copy-start.4
  238.4 4.7 copy-start.3
  244.4 8.4 %copy-start = (f32[4,512,128,8]{2,1,3,0:T(8,128)}, f32[4,512,128,8]{2,1,3,0:T(8,128)S(1)}, u32[]{:S(2)}) copy-start(f32[4,512,128,8]{2,1,3,0:T(8,128)S(1)} %fusion.45) | copy-start | bytes 25165828 | tf_op jit(solution)/shard_map/while/body/eval_jaxpr/cond
  252.8 2.7 copy-start.2
  271.9 6.6 copy-start.1
  287.8 4.7 copy-start.3
  293.8 8.4 %copy-start = (f32[4,512,128,8]{2,1,3,0:T(8,128)}, f32[4,512,128,8]{2,1,3,0:T(8,128)S(1)}, u32[]{:S(2)}) copy-start(f32[4,512,128,8]{2,1,3,0:T(8,128)S(1)} %fusion.45) | copy-start | bytes 25165828 | tf_op jit(solution)/shard_map/while/body/eval_jaxpr/cond
  302.2 2.7 copy-start.2
  321.3 6.6 copy-start.1
  337.2 4.7 copy-start.3
  343.2 8.4 %copy-start = (f32[4,512,128,8]{2,1,3,0:T(8,128)}, f32[4,512,128,8]{2,1,3,0:T(8,128)S(1)}, u32[]{:S(2)}) copy-start(f32[4,512,128,8]{2,1,3,0:T(8,128)S(1)} %fusion.45) | copy-start | bytes 25165828 | tf_op jit(solution)/shard_map/while/body/eval_jaxpr/cond
  351.6 2.7 copy-start.2
  370.7 6.6 copy-start.1
  386.5 4.7 copy-start.3
  392.5 8.4 %copy-start = (f32[4,512,128,8]{2,1,3,0:T(8,128)}, f32[4,512,128,8]{2,1,3,0:T(8,128)S(1)}, u32[]{:S(2)}) copy-start(f32[4,512,128,8]{2,1,3,0:T(8,128)S(1)} %fusion.45) | copy-start | bytes 25165828 | tf_op jit(solution)/shard_map/while/body/eval_jaxpr/cond
  401.0 2.7 copy-start.2
  420.0 6.6 copy-start.1
  444.7 0.7 copy-start.8
  444.7 225.8 %copy-start.5 = (bf16[1,128,2,512]{3,2,1,0:T(2,128)(2,1)S(1)}, bf16[1,128,2,512]{3,2,1,0:T(2,128)(2,1)}, u32[]{:S(2)}) copy-start(bf16[1,128,2,512]{3,2,1,0:T(2,128)(2,1)} %param.16) | copy-start | bytes 786436
Sparse Core Ops, SparseCore 0:
  11.1 79.9 all-gather.2
  93.7 74.2 all-gather.4
  444.8 225.5 all-reduce.2
where the time goes:
time: 766 us; the launch traced here: 765 us
  waiting for transfers between devices  371 us (48%)
  matrix products  212 us (28%)
  blocking collectives  80.5 us (11%)
  local copies, waits for them, and re-layouts  52.2 us (7%)
  other arithmetic  26.1 us (3%)
  between operations  16.3 us (2%)
    unnamed x4, waiting for transfers between devices  221 us
    psum x1, blocking collectives, on_device(): total_term = lax.psum(local_term, ('dp', 'context'))  80.5 us
    all_gather x1, waiting for transfers between devices, on_device(): lax.all_gather(key_tangents, 'context', axis=1, tiled=True)  76.8 us
    all_gather x1, waiting for transfers between devices, on_device(): lax.all_gather(keys_values, 'context', axis=1, tiled=True)  73.1 us
    dot_general x8, matrix products, products(): jnp.einsum('thgd,shd->hgts', output_adjoint, value_direction, preferred_e...  48.9 us
    dot_general x4, matrix products, grads_live(): jnp.einsum('hgts,thgd->shd', tprob_b, output_adjoint, preferred_element_t...  33.6 us
    dot_general x4, matrix products, grads_live(): jnp.einsum('hgts,shd->thgd', dscore_b, key_direction, preferred_element_t...  28.2 us
    dot_general x8, matrix products, products(): jnp.einsum('thgd,shd->hgts', output_adjoint, value_matrix, preferred_elem...  27.4 us
  transfers between devices with their start and end apart: 3, of which 3 were waited for; matrix products, arithmetic and copies ran while one was open for 2% of the time, Pallas kernels for 0%

commit v1 on v0

v1 whole, which is shorter than its diff:
```python
import functools

import jax
import jax.numpy as jnp
from jax import lax
from jax.experimental import pallas as pl
from jax.experimental.pallas import tpu as pltpu
from jax.sharding import PartitionSpec as P

HEAD = 128
QUERY_HEADS = 32
KV_HEADS = 4
TOK = 128
SPAN = 64
WINDOW = 2048
SHARDS = 16
HALF = 8
OWN_HEADS = 4
OWN_COLS = OWN_HEADS * HEAD
ROWS = OWN_HEADS * SPAN
TILE = 128
TILES = WINDOW // TILE
BLOCKS = WINDOW // SPAN
SCALE = float(HEAD) ** -0.5
LOG2E = 1.4426950408889634
EXP_SCALE = SCALE * LOG2E
SAFE_LOG2 = 60.0
MESH = pl.DeviceIdType.MESH
F32 = jnp.float32
BF16 = jnp.bfloat16


def coordinates():
    dp = lax.axis_index("dp")
    context = lax.axis_index("context")
    return dp, context // HALF, (context // 2) % 4, context % 2


def context_index(z_hi, y, core):
    return z_hi * HALF + y * 2 + core


def remote(src, dst, send, recv, device):
    return pltpu.make_async_remote_copy(
        src_ref=src, dst_ref=dst, send_sem=send, recv_sem=recv, device_id=device, device_id_type=MESH
    )


def enter(devices):
    barrier = pltpu.get_barrier_semaphore()
    for device in devices:
        pl.semaphore_signal(barrier, inc=1, device_id=device, device_id_type=MESH)
    pl.semaphore_wait(barrier, len(devices))


def columns_of(y, core):
    return pl.ds(pl.multiple_of((y * 2 + core) * OWN_COLS, OWN_COLS), OWN_COLS)


def spread_kernel(q, g, kv, q_out, g_out, kv_out, kv_send, sib_send, z_send, zsib_send, q_send, g_send, kv_recv, q_recv, g_recv, local):
    dp, zh, y, c = coordinates()
    me = context_index(zh, y, c)
    sibling = (dp, context_index(zh, y, 1 - c))
    across = (dp, context_index(1 - zh, y, c))
    peers = []
    for dy in (1, 3, 2, 0):
        for dc in (0, 1):
            if dy or dc:
                peers.append(((y + dy) % 4, (c + dc) % 2))
    enter([(dp, context_index(zh, py, pc)) for py, pc in peers] + [across])

    own = zh * HALF + y * 2 + c
    slot_here = y * 2 + c
    locals_ = [
        pltpu.make_async_copy(kv.at[y], kv_out.at[own], local.at[0]),
        pltpu.make_async_copy(q.at[:, columns_of(y, c)], q_out.at[slot_here], local.at[1]),
        pltpu.make_async_copy(g.at[:, columns_of(y, c)], g_out.at[slot_here], local.at[2]),
    ]
    copies = []

    def start(copy):
        copy.start()
        copies.append(copy)

    for n, dy in enumerate((1, 3, 2)):
        ty = (y + dy) % 4
        start(remote(kv.at[ty], kv_out.at[own], kv_send.at[n], kv_recv.at[own], (dp, context_index(zh, ty, c))))
    start(remote(kv.at[y], kv_out.at[own], z_send.at[0], kv_recv.at[own], across))
    start(remote(kv.at[y], kv_out.at[own], sib_send.at[0], kv_recv.at[own], sibling))
    for copy in locals_:
        copy.start()
    for n, dy in enumerate((1, 3, 2)):
        slot = context_index(zh, (y + 4 - dy) % 4, c)
        here = kv_out.at[slot]
        remote(here, here, kv_send.at[n], kv_recv.at[slot], across).wait_recv()
        start(remote(here, here, z_send.at[1 + n], kv_recv.at[slot], across))
        start(remote(here, here, sib_send.at[1 + n], kv_recv.at[slot], sibling))
    for n, (py, pc) in enumerate(peers):
        target = (dp, context_index(zh, py, pc))
        start(remote(q.at[:, columns_of(py, pc)], q_out.at[slot_here], q_send.at[n], q_recv.at[slot_here], target))
        start(remote(g.at[:, columns_of(py, pc)], g_out.at[slot_here], g_send.at[n], g_recv.at[slot_here], target))
    for n, dy in enumerate((0, 1, 3, 2)):
        slot = context_index(1 - zh, (y + 4 - dy) % 4, c)
        here = kv_out.at[slot]
        remote(here, here, z_send.at[n], kv_recv.at[slot], across).wait_recv()
        start(remote(here, here, zsib_send.at[n], kv_recv.at[slot], sibling))
    for z in range(2):
        for ys in range(4):
            slot = context_index(z, ys, 1 - c)
            here = kv_out.at[slot]
            remote(here, here, z_send.at[0], kv_recv.at[slot], sibling).wait_recv()
    for n, (py, pc) in enumerate(peers):
        slot = py * 2 + pc
        remote(q_out.at[slot], q_out.at[slot], q_send.at[n], q_recv.at[slot], sibling).wait_recv()
        remote(g_out.at[slot], g_out.at[slot], g_send.at[n], g_recv.at[slot], sibling).wait_recv()
    for copy in copies:
        copy.wait_send()
    for copy in locals_:
        copy.wait()


def spread(q, g, kv):
    any_ = pl.BlockSpec(memory_space=pl.ANY)
    dma = pltpu.SemaphoreType.DMA
    return pl.pallas_call(
        spread_kernel,
        out_shape=(
            jax.ShapeDtypeStruct((HALF, TOK, OWN_COLS), BF16),
            jax.ShapeDtypeStruct((HALF, TOK, OWN_COLS), BF16),
            jax.ShapeDtypeStruct((SHARDS, 4, TOK, HEAD), BF16),
        ),
        in_specs=[any_] * 3,
        out_specs=(any_,) * 3,
        scratch_shapes=[
            dma((3,)), dma((4,)), dma((4,)), dma((4,)), dma((7,)), dma((7,)),
            dma((SHARDS,)), dma((HALF,)), dma((HALF,)), dma((3,)),
        ],
        compiler_params=pltpu.CompilerParams(collective_id=0, has_side_effects=True),
        name="spread",
    )(q, g, kv)


def nt_dot(a, b):
    return lax.dot_general(a, b, (((1,), (1,)), ((), ())), preferred_element_type=F32)


def nn_dot(a, b):
    return jnp.dot(a, b, preferred_element_type=F32)


def fold_rows(x):
    return jnp.sum(x.reshape(x.shape[0] // 8, 8, x.shape[1]), axis=0)


def hvp_kernel(pair, seg, q, g, kv, hq_out, hkv_out, curv_out, kt, vt, kt_t, hk_acc, hv_acc, hq_acc):
    _, zh, _, _ = coordinates()
    segments = seg[...]
    starts = [jnp.sum((segments < d).astype(jnp.int32)) for d in (1, 2, 3)]

    ones = jnp.ones((HEAD, HEAD), BF16)

    def prepare(i, carry):
        first = pair[i]
        for half in range(2):
            block = first if half == 0 else BLOCKS - 1 - first
            tile = block // (TILE // SPAN)
            off = pl.multiple_of((block % (TILE // SPAN)) * SPAN, SPAN)
            rows = pl.ds(half * SPAN, SPAN)
            k = kv[i, 0, rows, :]
            kt[tile, pl.ds(off, SPAN), :] = k
            kt[tile, pl.ds(off + TILE, SPAN), :] = kv[i, 2, rows, :]
            vt[tile, pl.ds(off, SPAN), :] = kv[i, 1, rows, :]
            vt[tile, pl.ds(off + TILE, SPAN), :] = kv[i, 3, rows, :]
            k32 = k.astype(F32)
            carry = jnp.maximum(carry, fold_max(nn_dot((k32 * k32).astype(BF16), ones)))
        return carry

    def fold_max(x):
        return jnp.max(x.reshape(x.shape[0] // 8, 8, x.shape[1]), axis=0)

    key_norm = lax.fori_loop(0, SHARDS, prepare, jnp.zeros((8, HEAD), F32))

    def transpose_tile(t, carry):
        both = kt[t].astype(F32)
        kt_t[t, :, 0:TILE] = both[:TILE].T.astype(BF16)
        kt_t[t, :, TILE:] = both[TILE:].T.astype(BF16)
        hk_acc[t] = jnp.zeros((TILE, HEAD), F32)
        hv_acc[t] = jnp.zeros((TILE, HEAD), F32)
        return carry

    lax.fori_loop(0, TILES, transpose_tile, 0)

    def query_norms(s, carry):
        for h in range(OWN_HEADS):
            x = q[s, :, h * HEAD:(h + 1) * HEAD].astype(F32)
            carry = jnp.maximum(carry, fold_max(nn_dot((x * x).astype(BF16), ones)))
        return carry

    query_norm = lax.fori_loop(0, HALF, query_norms, jnp.zeros((8, HEAD), F32))
    bound = jnp.max(key_norm) * jnp.max(query_norm) * (EXP_SCALE * EXP_SCALE)
    safe = bound < SAFE_LOG2 * SAFE_LOG2

    lane = lax.broadcasted_iota(jnp.int32, (1, ROWS), 1)
    key_row = lax.broadcasted_iota(jnp.int32, (TILE, 1), 0)

    def query_block(n, carry):
        s = n // 2
        half = n % 2
        first = pair[zh * HALF + s]
        block = jnp.where(half == 0, first, BLOCKS - 1 - first)
        base = block * SPAN
        rows = pl.ds(pl.multiple_of(half * SPAN, SPAN), SPAN)
        qb = jnp.concatenate([q[s, rows, h * HEAD:(h + 1) * HEAD] for h in range(OWN_HEADS)], axis=0)
        gb = jnp.concatenate([g[s, rows, h * HEAD:(h + 1) * HEAD] for h in range(OWN_HEADS)], axis=0)
        query_pos = base + lane % SPAN
        doc_start = jnp.zeros_like(query_pos)
        low = jnp.int32(0)
        for start in starts:
            doc_start = jnp.where(query_pos >= start, start, doc_start)
            low = jnp.where(base >= start, start, low)
        first_tile = low // TILE
        last_tile = base // TILE + 1

        def seen_in(t):
            key_pos = t * TILE + key_row
            return (key_pos >= doc_start) & (key_pos <= query_pos)

        def peak_pass(_):
            def step(t, top):
                logits = nt_dot(kt[t, :TILE], qb) * EXP_SCALE
                masked = jnp.where(seen_in(t), logits, -1e30)
                return jnp.maximum(top, fold_max(masked))
            top = lax.fori_loop(first_tile, last_tile, step, jnp.full((8, ROWS), -1e30, F32))
            return jnp.max(top, axis=0, keepdims=True)

        peak = lax.cond(safe, lambda _: jnp.zeros((1, ROWS), F32), peak_pass, 0)

        def stats_step(t, carry):
            total, mu, delta, mixed = carry
            st = nt_dot(kt[t], qb)
            dt = nt_dot(vt[t], gb)
            w = jnp.where(seen_in(t), jnp.exp2(st[:TILE] * EXP_SCALE - peak), 0.0)
            ts = st[TILE:] * SCALE
            dprob = dt[:TILE]
            total = total + fold_rows(w)
            mu = mu + fold_rows(w * ts)
            delta = delta + fold_rows(w * dprob)
            mixed = mixed + fold_rows(w * (ts * dprob + dt[TILE:]))
            return total, mu, delta, mixed

        zero = jnp.zeros((8, ROWS), F32)
        sums = lax.fori_loop(first_tile, last_tile, stats_step, (zero,) * 4)
        total, mu, delta, mixed = [jnp.sum(x, axis=0, keepdims=True) for x in sums]
        inverse = 1.0 / total
        mu = mu * inverse
        delta = delta * inverse
        tdelta = mixed * inverse - mu * delta
        level = peak + jnp.log2(total)

        hq_acc[...] = jnp.zeros_like(hq_acc)

        def grads_step(t, carry):
            st = nt_dot(kt[t], qb)
            dt = nt_dot(vt[t], gb)
            prob = jnp.where(seen_in(t), jnp.exp2(st[:TILE] * EXP_SCALE - level), 0.0)
            tsc = st[TILE:] * SCALE - mu
            dpc = dt[:TILE] - delta
            tdc = dt[TILE:] - tdelta
            tp = (prob * tsc).astype(BF16)
            ds = (prob * dpc).astype(BF16)
            tds = (prob * (tsc * dpc + tdc)).astype(BF16)
            hk_acc[t] += nn_dot(tds, qb)
            hv_acc[t] += nn_dot(tp, gb)
            hq_acc[...] += nn_dot(kt_t[t], jnp.concatenate([tds, ds], axis=0))
            return carry

        lax.fori_loop(first_tile, last_tile, grads_step, 0)
        hq = (hq_acc[...] * SCALE).T.astype(BF16)
        for h in range(OWN_HEADS):
            hq_out[s, rows, h * HEAD:(h + 1) * HEAD] = hq[h * SPAN:(h + 1) * SPAN]
        return carry

    lax.fori_loop(0, 2 * HALF, query_block, 0)

    def finish(i, carry):
        first = pair[i]
        for half in range(2):
            block = first if half == 0 else BLOCKS - 1 - first
            tile = block // (TILE // SPAN)
            off = pl.multiple_of((block % (TILE // SPAN)) * SPAN, SPAN)
            rows = pl.ds(half * SPAN, SPAN)
            hk = hk_acc[tile, pl.ds(off, SPAN), :] * SCALE
            hv = hv_acc[tile, pl.ds(off, SPAN), :]
            carry = carry + fold_rows(kv[i, 2, rows, :].astype(F32) * hk)
            carry = carry + fold_rows(kv[i, 3, rows, :].astype(F32) * hv)
            z = i // HALF
            ys = (i // 2) % 4
            core = i % 2
            hkv_out[core, z, ys, 0, rows, :] = hk.astype(BF16)
            hkv_out[core, z, ys, 1, rows, :] = hv.astype(BF16)
        return carry

    curv = lax.fori_loop(0, SHARDS, finish, jnp.zeros((8, HEAD), F32))
    curv_out[...] = jnp.full((8, HEAD), jnp.sum(curv), F32)


def hvp(pair, seg, q, g, kv):
    vmem = pl.BlockSpec(memory_space=pltpu.VMEM)
    return pl.pallas_call(
        hvp_kernel,
        out_shape=(
            jax.ShapeDtypeStruct((HALF, TOK, OWN_COLS), BF16),
            jax.ShapeDtypeStruct((2, 2, 4, 2, TOK, HEAD), BF16),
            jax.ShapeDtypeStruct((8, HEAD), F32),
        ),
        in_specs=[pl.BlockSpec(memory_space=pltpu.SMEM)] + [vmem] * 4,
        out_specs=(vmem,) * 3,
        scratch_shapes=[
            pltpu.VMEM((TILES, 2 * TILE, HEAD), BF16),
            pltpu.VMEM((TILES, 2 * TILE, HEAD), BF16),
            pltpu.VMEM((TILES, HEAD, 2 * TILE), BF16),
            pltpu.VMEM((TILES, TILE, HEAD), F32),
            pltpu.VMEM((TILES, TILE, HEAD), F32),
            pltpu.VMEM((HEAD, ROWS), F32),
        ],
        compiler_params=pltpu.CompilerParams(vmem_limit_bytes=50 << 20),
        name="hvp",
    )(pair, seg, q, g, kv)


def collect_kernel(hq, hkv, curv, hq_out, hkv_out, curv_out, sib_buf, z_buf, z_stage, y_stage, a_buf, b_buf, c_buf, b_own, c_own, hq_send, hq_recv, sib_send, sib_recv, z_send, z_recv, y_send, y_recv, a_send, a_recv, b_send, b_recv, c_send, c_recv, local):
    dp, zh, y, c = coordinates()
    x = dp % 4
    z_lo = dp // 4
    z = zh * 4 + z_lo
    sibling = (dp, context_index(zh, y, 1 - c))
    across = (dp, context_index(1 - zh, y, c))
    peers = []
    for dy in (1, 3, 2, 0):
        for dc in (0, 1):
            if dy or dc:
                peers.append(((y + dy) % 4, (c + dc) % 2))
    row_devices = [(dp, context_index(zh, py, pc)) for py, pc in peers]
    z_peers = [(z + dz) % 8 for dz in range(1, 8)]
    z_devices = [((pz % 4) * 4 + x, context_index(pz // 4, y, c)) for pz in z_peers]
    x_peers = [(x + dx) % 4 for dx in range(1, 4)]
    x_devices = [(z_lo * 4 + px, context_index(zh, y, c)) for px in x_peers]
    enter(row_devices + z_devices + x_devices)

    copies = []

    def start(copy):
        copy.start()
        copies.append(copy)

    slot_here = y * 2 + c
    for n, which in enumerate((1 - zh, zh)):
        start(remote(hkv.at[1 - c, which], sib_buf.at[which], sib_send.at[n], sib_recv.at[n], sibling))
    for n, device in enumerate(row_devices):
        start(remote(curv, a_buf.at[slot_here], a_send.at[n], a_recv.at[slot_here], device))
    for n, (py, pc) in enumerate(peers):
        start(remote(hq.at[py * 2 + pc], hq_out.at[:, columns_of(y, c)], hq_send.at[n], hq_recv.at[slot_here], row_devices[n]))
    own_hq = pltpu.make_async_copy(hq.at[slot_here], hq_out.at[:, columns_of(y, c)], local.at[0])
    own_hq.start()

    other = 1 - zh
    remote(sib_buf.at[other], sib_buf.at[other], sib_send.at[0], sib_recv.at[0], sibling).wait_recv()
    for ys in range(4):
        for part in range(2):
            z_stage[ys, part] = (hkv[c, other, ys, part].astype(F32) + sib_buf[other, ys, part].astype(F32)).astype(BF16)
    start(remote(z_stage, z_buf, z_send, z_recv, across))

    for n, (py, pc) in enumerate(peers):
        slot = py * 2 + pc
        remote(a_buf.at[slot], a_buf.at[slot], a_send.at[n], a_recv.at[slot], sibling).wait_recv()
    a_buf[slot_here] = curv[...]
    b_own[...] = jnp.sum(a_buf[...], axis=0)
    for n, device in enumerate(z_devices):
        start(remote(b_own, b_buf.at[z], b_send.at[n], b_recv.at[z], device))
    for n, pz in enumerate(z_peers):
        remote(b_buf.at[pz], b_buf.at[pz], b_send.at[n], b_recv.at[pz], sibling).wait_recv()
    b_buf[z] = b_own[...]
    c_own[...] = jnp.sum(b_buf[...], axis=0)
    for n, device in enumerate(x_devices):
        start(remote(c_own, c_buf.at[x], c_send.at[n], c_recv.at[x], device))
    for n, px in enumerate(x_peers):
        remote(c_buf.at[px], c_buf.at[px], c_send.at[n], c_recv.at[px], sibling).wait_recv()
    c_buf[x] = c_own[...]
    curv_out[...] = jnp.sum(c_buf[...], axis=0) * (1.0 / (SHARDS * WINDOW))

    remote(sib_buf.at[zh], sib_buf.at[zh], sib_send.at[1], sib_recv.at[1], sibling).wait_recv()
    remote(z_stage, z_buf, z_send, z_recv, across).wait_recv()
    for ys in range(4):
        for part in range(2):
            total = hkv[c, zh, ys, part].astype(F32) + sib_buf[zh, ys, part].astype(F32) + z_buf[ys, part].astype(F32)
            y_stage[ys, part] = total.astype(BF16)
    for n, dy in enumerate((1, 3, 2)):
        ty = (y + dy) % 4
        start(remote(y_stage.at[ty], hkv_out.at[y], y_send.at[n], y_recv.at[y], (dp, context_index(zh, ty, c))))
    own_kv = pltpu.make_async_copy(y_stage.at[y], hkv_out.at[y], local.at[1])
    own_kv.start()
    for n, dy in enumerate((1, 3, 2)):
        ty = (y + dy) % 4
        remote(hkv_out.at[ty], hkv_out.at[ty], y_send.at[n], y_recv.at[ty], sibling).wait_recv()
    for n, (py, pc) in enumerate(peers):
        slot = py * 2 + pc
        remote(hq.at[slot], hq_out.at[:, columns_of(py, pc)], hq_send.at[n], hq_recv.at[slot], sibling).wait_recv()
    for copy in copies:
        copy.wait_send()
    own_hq.wait()
    own_kv.wait()


def collect(hq, hkv, curv):
    vmem = pl.BlockSpec(memory_space=pltpu.VMEM)
    any_ = pl.BlockSpec(memory_space=pl.ANY)
    dma = pltpu.SemaphoreType.DMA
    return pl.pallas_call(
        collect_kernel,
        out_shape=(
            jax.ShapeDtypeStruct((TOK, QUERY_HEADS * HEAD), BF16),
            jax.ShapeDtypeStruct((KV_HEADS, 2, TOK, HEAD), BF16),
            jax.ShapeDtypeStruct((8, HEAD), F32),
        ),
        in_specs=[any_, vmem, vmem],
        out_specs=(any_, any_, vmem),
        scratch_shapes=[
            pltpu.VMEM((2, 4, 2, TOK, HEAD), BF16),
            pltpu.VMEM((4, 2, TOK, HEAD), BF16),
            pltpu.VMEM((4, 2, TOK, HEAD), BF16),
            pltpu.VMEM((4, 2, TOK, HEAD), BF16),
            pltpu.VMEM((HALF, 8, HEAD), F32),
            pltpu.VMEM((8, 8, HEAD), F32),
            pltpu.VMEM((4, 8, HEAD), F32),
            pltpu.VMEM((8, HEAD), F32),
            pltpu.VMEM((8, HEAD), F32),
            dma((7,)), dma((HALF,)), dma((2,)), dma((2,)), dma, dma, dma((3,)), dma((4,)),
            dma((7,)), dma((HALF,)), dma((7,)), dma((8,)), dma((3,)), dma((4,)), dma((2,)),
        ],
        compiler_params=pltpu.CompilerParams(collective_id=1, has_side_effects=True, vmem_limit_bytes=24 << 20),
        name="collect",
    )(hq, hkv, curv)


def on_device(queries, keys_values, key_tangents, output_adjoint_rows, segments, span_pair):
    kv = jnp.concatenate([keys_values[0], key_tangents[0]], axis=1)
    kv = kv.reshape(TOK, 4, KV_HEADS, HEAD).transpose(2, 1, 0, 3)
    q, g, kv = spread(queries[0], output_adjoint_rows[0], kv)
    hq, hkv, curv = hvp(span_pair, segments.reshape(SHARDS, TOK), q, g, kv)
    hq, hkv, curv = collect(hq, hkv, curv)
    hkv = hkv.transpose(2, 1, 0, 3).reshape(1, TOK, 2, KV_HEADS * HEAD)
    return hq[None], hkv, curv[0, 0]


def solution(mesh):
    in_specs = (
        P("dp", "context", None),
        P("dp", "context", None, None),
        P("dp", "context", None, None),
        P("dp", "context", None),
        P("dp", None),
        P(),
    )
    out_specs = (P("dp", "context", None), P("dp", "context", None, None), P())
    return jax.shard_map(on_device, mesh=mesh, in_specs=in_specs, out_specs=out_specs, check_vma=False)
```

time: 766 us -> 178 us (0.23)
  waiting for transfers between devices: 371 us -> 0 us
  matrix products: 212 us -> 0 us
  Pallas kernels: 0 us -> 170 us
  blocking collectives: 80.5 us -> 0 us
  local copies, waits for them, and re-layouts: 52.2 us -> 6.44 us
  other arithmetic: 26.1 us -> 0.84 us
  between operations: 16.3 us -> 0.72 us
    unnamed x4 -> x0, waiting for transfers between devices: 221 us -> none
    dot_general x48 -> x0, matrix products: 212 us -> none  [the longest x8 48.9 us: products(): jnp.einsum('thgd,shd->hgts', output_adjoint, value_direction, preferred_e...]
    pallas_call x0 -> x3, Pallas kernels: none -> 170 us  [the longest x1 88 us: hvp(): pl.pallas_call(hvp_kernel, out_shape=(jax.ShapeDtypeStruct((HALF, TOK, OW...]
    all_gather x2 -> x0, waiting for transfers between devices: 150 us -> none  [the longest x1 76.8 us: on_device(): lax.all_gather(key_tangents, 'context', axis=1, tiled=True)]
    psum x1 -> x0, blocking collectives: 80.5 us -> none  [on_device(): total_term = lax.psum(local_term, ('dp', 'context'))]
    slice x8 -> x1, local copies, waits for them, and re-layouts: 17.4 us -> 0.51 us  [on_device(): return (hq[None], hkv, curv[0, 0])]
    while x3 -> x0, local copies, waits for them, and re-layouts: 16.1 us -> none  [sweep(): return lax.fori_loop(0, turns, turn, init)]
    dynamic_update_slice x4 -> x0, other arithmetic: 13.8 us -> none  [grads_live(): key_acc = lax.dynamic_update_slice_in_dim(key_acc, old + block, start, 0)]
  transfers between devices with their start and end apart: 3 -> 0, of which waited for: 3 -> 0; matrix products, arithmetic and copies ran while one was open for 2% -> 0% of each run, Pallas kernels for 0% -> 0%
where the time goes in v1:
time: 178 us
  Pallas kernels  170 us (96%)
  local copies, waits for them, and re-layouts  6.44 us (4%)
    pallas_call x1, Pallas kernels, hvp(): pl.pallas_call(hvp_kernel, out_shape=(jax.ShapeDtypeStruct((HALF, TOK, OW...  88 us
    pallas_call x1, Pallas kernels, collect(): pl.pallas_call(collect_kernel, out_shape=(jax.ShapeDtypeStruct((TOK, QUER...  43.1 us
    pallas_call x1, Pallas kernels, spread(): pl.pallas_call(spread_kernel, out_shape=(jax.ShapeDtypeStruct((HALF, TOK,...  38.6 us
    unnamed x10, local copies, waits for them, and re-layouts  5.39 us

profile of v1, /device:TPU:32, one launch (start us, length us, event | category | flops | bytes accessed | tf_op | source)
XLA Modules:
  0.0 177.7 jit_solution(11966335958649791487)
XLA Ops:
  0.6 1.2 copy.9
  1.8 0.2 copy.11
  2.0 1.2 copy.10
  3.1 0.0 copy-start.1
  3.1 0.0 copy-start.2
  3.1 0.2 copy.12
  3.3 0.8 maximum_bitcast_fusion.kv
  4.2 38.6 %spread.1 = (bf16[8,128,512]{2,1,0:T(8,128)(2,1)}, bf16[8,128,512]{2,1,0:T(8,128)(2,1)}, bf16[16,4,128,128]{3,2,1,0:T(8,128)(2,1)}) custom-call(bf16[128,4096]{1,0:T(8,128)(2,1)} %bitcast.14, bf16[128,4096]{1,0:T(8,128)(2,1)} %bitcast.15, bf16[4,4,128,128]{3,2,1,0:T(8,128)(2,1)} %maximum_bitcast_fusion.kv), custom_call_target="tpu_custom_call" | custom-call | tf_op jit(solution)/shard_map/spread/pallas_call | solution.py:125
  42.7 0.0 copy-done.1
  42.7 0.0 copy-done.2
  42.8 0.0 copy-start
  42.8 1.2 copy-done
  44.0 88.0 %hvp.1 = (bf16[8,128,512]{2,1,0:T(8,128)(2,1)S(1)}, bf16[2,2,4,2,128,128]{5,4,3,2,1,0:T(8,128)(2,1)S(1)}, f32[8,128]{1,0:T(8,128)S(1)}) custom-call(s32[16]{0:T(128)S(1)} %copy-done.2, s32[16,128]{1,0:T(8,128)S(1)} %bitcast.13, bf16[8,128,512]{2,1,0:T(8,128)(2,1)S(1)} %copy-done, bf16[8,128,512]{2,1,0:T(8,128)(2,1)} %get-tuple-element.13.g, ...), custom_call_target="tpu_custom_call" | custom-call | tf_op jit(solution)/shard_map/hvp/pallas_call | solution.py:309
  132.0 43.1 %collect.1 = (bf16[128,4096]{1,0:T(8,128)(2,1)S(1)}, bf16[4,2,128,128]{3,2,1,0:T(8,128)(2,1)S(1)}, f32[8,128]{1,0:T(8,128)S(1)}) custom-call(bf16[8,128,512]{2,1,0:T(8,128)(2,1)S(1)} %get-tuple-element.15.hq, bf16[2,2,4,2,128,128]{5,4,3,2,1,0:T(8,128)(2,1)S(1)} %get-tuple-element.16.hkv, f32[8,128]{1,0:T(8,128)S(1)} %get-tuple-element.17.curv), custom_call_target="tpu_custom_call" | custom-call | tf_op jit(solution)/shard_map/collect/pallas_call | solution.py:418
  175.1 0.5 slice.3
  175.7 0.2 copy.13
  175.8 0.9 copy.14
  176.7 1.0 copy.16
Async XLA Ops:
  3.1 39.6 %copy-start.1 = (s32[1,2048]{1,0:T(1,128)S(1)}, s32[1,2048]{1,0:T(1,128)}, u32[]{:S(2)}) copy-start(s32[1,2048]{1,0:T(1,128)} %param.10) | copy-start | bytes 24580
  3.1 39.6 %copy-start.2 = (s32[16]{0:T(128)S(1)}, s32[16]{0:T(128)}, u32[]{:S(2)}) copy-start(s32[16]{0:T(128)} %pair.1) | copy-start | bytes 196
  42.8 1.2 copy-start

commit v2 on v1

--- a/solution.py
+++ b/solution.py
@@ -18,9 +18,10 @@
 OWN_HEADS = 4
 OWN_COLS = OWN_HEADS * HEAD
 ROWS = OWN_HEADS * SPAN
-TILE = 128
+TILE = 256
 TILES = WINDOW // TILE
 BLOCKS = WINDOW // SPAN
+CHUNKS = TILE // SPAN
 SCALE = float(HEAD) ** -0.5
 LOG2E = 1.4426950408889634
 EXP_SCALE = SCALE * LOG2E
@@ -152,43 +153,54 @@
     return jnp.sum(x.reshape(x.shape[0] // 8, 8, x.shape[1]), axis=0)
 
 
-def hvp_kernel(pair, seg, q, g, kv, hq_out, hkv_out, curv_out, kt, vt, kt_t, hk_acc, hv_acc, hq_acc):
+def hvp_kernel(pair, seg, q, g, kv, hq_out, hkv_out, curv_out, kt, vt, k_t, tk_t, qt, gt, q_rows, g_rows, even, odd, p_even, p_odd, hk_acc, hv_acc, hq_acc):
     _, zh, _, _ = coordinates()
     segments = seg[...]
     starts = [jnp.sum((segments < d).astype(jnp.int32)) for d in (1, 2, 3)]
 
     ones = jnp.ones((HEAD, HEAD), BF16)
+
+    def fold_max(x):
+        return jnp.max(x.reshape(x.shape[0] // 8, 8, x.shape[1]), axis=0)
+
+    def split_into(row, x):
+        high = x.astype(BF16)
+        kt[pl.ds(row, SPAN), 0:HEAD] = high
+        kt[pl.ds(row, SPAN), HEAD:] = (x - high.astype(F32)).astype(BF16)
+
+    def key_place(block):
+        tile = block // CHUNKS
+        return pl.multiple_of(tile * (2 * TILE) + (block % CHUNKS) * SPAN, SPAN)
 
     def prepare(i, carry):
         first = pair[i]
         for half in range(2):
             block = first if half == 0 else BLOCKS - 1 - first
-            tile = block // (TILE // SPAN)
-            off = pl.multiple_of((block % (TILE // SPAN)) * SPAN, SPAN)
+            row = key_place(block)
             rows = pl.ds(half * SPAN, SPAN)
-            k = kv[i, 0, rows, :]
-            kt[tile, pl.ds(off, SPAN), :] = k
-            kt[tile, pl.ds(off + TILE, SPAN), :] = kv[i, 2, rows, :]
-            vt[tile, pl.ds(off, SPAN), :] = kv[i, 1, rows, :]
-            vt[tile, pl.ds(off + TILE, SPAN), :] = kv[i, 3, rows, :]
-            k32 = k.astype(F32)
-            carry = jnp.maximum(carry, fold_max(nn_dot((k32 * k32).astype(BF16), ones)))
+            k = kv[i, 0, rows, :].astype(F32)
+            tk = kv[i, 2, rows, :].astype(F32)
+            split_into(row, k * EXP_SCALE)
+            split_into(row + TILE, tk * SCALE)
+            vt[pl.ds(row, SPAN), :] = kv[i, 1, rows, :]
+            vt[pl.ds(row + TILE, SPAN), :] = kv[i, 3, rows, :]
+            here = pl.ds(pl.multiple_of(block * SPAN, SPAN), SPAN)
+            hk_acc[here, :] = k
+            hv_acc[here, :] = tk
+            carry = jnp.maximum(carry, fold_max(nn_dot((k * k).astype(BF16), ones)))
         return carry
 
-    def fold_max(x):
-        return jnp.max(x.reshape(x.shape[0] // 8, 8, x.shape[1]), axis=0)
-
     key_norm = lax.fori_loop(0, SHARDS, prepare, jnp.zeros((8, HEAD), F32))
 
-    def transpose_tile(t, carry):
-        both = kt[t].astype(F32)
-        kt_t[t, :, 0:TILE] = both[:TILE].T.astype(BF16)
-        kt_t[t, :, TILE:] = both[TILE:].T.astype(BF16)
-        hk_acc[t] = jnp.zeros((TILE, HEAD), F32)
-        hv_acc[t] = jnp.zeros((TILE, HEAD), F32)
+    def turn(t, carry):
+        here = pl.ds(pl.multiple_of(t * TILE, TILE), TILE)
+        k_t[:, here] = hk_acc[here, :].T.astype(BF16)
+        tk_t[:, here] = hv_acc[here, :].T.astype(BF16)
+        hk_acc[here, :] = jnp.zeros((TILE, HEAD), F32)
+        hv_acc[here, :] = jnp.zeros((TILE, HEAD), F32)
         return carry
 
-    lax.fori_loop(0, TILES, transpose_tile, 0)
+    lax.fori_loop(0, TILES, turn, 0)
 
     def query_norms(s, carry):
         for h in range(OWN_HEADS):
@@ -201,7 +213,7 @@
     safe = bound < SAFE_LOG2 * SAFE_LOG2
 
     lane = lax.broadcasted_iota(jnp.int32, (1, ROWS), 1)
-    key_row = lax.broadcasted_iota(jnp.int32, (TILE, 1), 0)
+    key_row = lax.broadcasted_iota(jnp.int32, (SPAN, ROWS), 0)
 
     def query_block(n, carry):
         s = n // 2
@@ -210,8 +222,15 @@
         block = jnp.where(half == 0, first, BLOCKS - 1 - first)
         base = block * SPAN
         rows = pl.ds(pl.multiple_of(half * SPAN, SPAN), SPAN)
-        qb = jnp.concatenate([q[s, rows, h * HEAD:(h + 1) * HEAD] for h in range(OWN_HEADS)], axis=0)
-        gb = jnp.concatenate([g[s, rows, h * HEAD:(h + 1) * HEAD] for h in range(OWN_HEADS)], axis=0)
+        for h in range(OWN_HEADS):
+            cols = slice(h * HEAD, (h + 1) * HEAD)
+            part = slice(h * SPAN, (h + 1) * SPAN)
+            q_rows[part, :] = q[s, rows, cols]
+            g_rows[part, :] = g[s, rows, cols]
+        qt_half = q_rows[...].astype(F32).T.astype(BF16)
+        qt[0:HEAD, :] = qt_half
+        qt[HEAD:, :] = qt_half
+        gt[...] = g_rows[...].astype(F32).T.astype(BF16)
         query_pos = base + lane % SPAN
         doc_start = jnp.zeros_like(query_pos)
         low = jnp.int32(0)
@@ -219,62 +238,108 @@
             doc_start = jnp.where(query_pos >= start, start, doc_start)
             low = jnp.where(base >= start, start, low)
         first_tile = low // TILE
-        last_tile = base // TILE + 1
-
-        def seen_in(t):
-            key_pos = t * TILE + key_row
-            return (key_pos >= doc_start) & (key_pos <= query_pos)
+        tiles = base // TILE + 1 - first_tile
+        pairs = (tiles - 1) // 2
+        oldest = doc_start - first_tile * TILE
+        newest = query_pos - first_tile * TILE
+
+        def seen_in(r, c):
+            key_pos = r * TILE + c * SPAN + key_row
+            return (key_pos >= oldest) & (key_pos <= newest)
+
+        def key_rows(t):
+            return pl.ds(pl.multiple_of(t * (2 * TILE), 2 * TILE), 2 * TILE)
 
         def peak_pass(_):
-            def step(t, top):
-                logits = nt_dot(kt[t, :TILE], qb) * EXP_SCALE
-                masked = jnp.where(seen_in(t), logits, -1e30)
-                return jnp.maximum(top, fold_max(masked))
-            top = lax.fori_loop(first_tile, last_tile, step, jnp.full((8, ROWS), -1e30, F32))
+            def step(r, top):
+                st = nn_dot(kt[key_rows(first_tile + r), :], qt[...])
+                for c in range(CHUNKS):
+                    masked = jnp.where(seen_in(r, c), st[c * SPAN:(c + 1) * SPAN], -1e30)
+                    top = jnp.maximum(top, fold_max(masked))
+                return top
+            top = lax.fori_loop(0, tiles, step, jnp.full((8, ROWS), -1e30, F32))
             return jnp.max(top, axis=0, keepdims=True)
 
         peak = lax.cond(safe, lambda _: jnp.zeros((1, ROWS), F32), peak_pass, 0)
 
-        def stats_step(t, carry):
+        def multiply(r, store):
+            where = key_rows(first_tile + r)
+            store[r // 2, 0] = nn_dot(kt[where, :], qt[...])
+            store[r // 2, 1] = nn_dot(vt[where, :], gt[...])
+
+        def tally(r, store, carry):
             total, mu, delta, mixed = carry
-            st = nt_dot(kt[t], qb)
-            dt = nt_dot(vt[t], gb)
-            w = jnp.where(seen_in(t), jnp.exp2(st[:TILE] * EXP_SCALE - peak), 0.0)
-            ts = st[TILE:] * SCALE
-            dprob = dt[:TILE]
-            total = total + fold_rows(w)
-            mu = mu + fold_rows(w * ts)
-            delta = delta + fold_rows(w * dprob)
-            mixed = mixed + fold_rows(w * (ts * dprob + dt[TILE:]))
+            for c in range(CHUNKS):
+                a = slice(c * SPAN, (c + 1) * SPAN)
+                b = slice(TILE + c * SPAN, TILE + (c + 1) * SPAN)
+                w = jnp.where(seen_in(r, c), jnp.exp2(store[r // 2, 0, a] - peak), 0.0)
+                store[r // 2, 0, a] = w
+                ts = store[r // 2, 0, b]
+                dprob = store[r // 2, 1, a]
+                total = total + fold_rows(w)
+                mu = mu + fold_rows(w * ts)
+                delta = delta + fold_rows(w * dprob)
+                mixed = mixed + fold_rows(w * (ts * dprob + store[r // 2, 1, b]))
             return total, mu, delta, mixed
 
+        def stats_pair(u, carry):
+            multiply(2 * u + 1, odd)
+            carry = tally(2 * u, even, carry)
+            multiply(2 * u + 2, even)
+            return tally(2 * u + 1, odd, carry)
+
+        def stats_two(carry):
+            multiply(tiles - 1, odd)
+            return tally(tiles - 1, odd, tally(tiles - 2, even, carry))
+
         zero = jnp.zeros((8, ROWS), F32)
-        sums = lax.fori_loop(first_tile, last_tile, stats_step, (zero,) * 4)
+        multiply(0, even)
+        sums = lax.fori_loop(0, pairs, stats_pair, (zero,) * 4)
+        one_left = tiles % 2 == 1
+        sums = lax.cond(one_left, functools.partial(tally, tiles - 1, even), stats_two, sums)
         total, mu, delta, mixed = [jnp.sum(x, axis=0, keepdims=True) for x in sums]
         inverse = 1.0 / total
         mu = mu * inverse
         delta = delta * inverse
         tdelta = mixed * inverse - mu * delta
-        level = peak + jnp.log2(total)
 
         hq_acc[...] = jnp.zeros_like(hq_acc)
 
-        def grads_step(t, carry):
-            st = nt_dot(kt[t], qb)
-            dt = nt_dot(vt[t], gb)
-            prob = jnp.where(seen_in(t), jnp.exp2(st[:TILE] * EXP_SCALE - level), 0.0)
-            tsc = st[TILE:] * SCALE - mu
-            dpc = dt[:TILE] - delta
-            tdc = dt[TILE:] - tdelta
-            tp = (prob * tsc).astype(BF16)
-            ds = (prob * dpc).astype(BF16)
-            tds = (prob * (tsc * dpc + tdc)).astype(BF16)
-            hk_acc[t] += nn_dot(tds, qb)
-            hv_acc[t] += nn_dot(tp, gb)
-            hq_acc[...] += nn_dot(kt_t[t], jnp.concatenate([tds, ds], axis=0))
+        def weigh(r, store, ready):
+            for c in range(CHUNKS):
+                a = slice(c * SPAN, (c + 1) * SPAN)
+                b = slice(TILE + c * SPAN, TILE + (c + 1) * SPAN)
+                prob = store[r // 2, 0, a] * inverse
+                tsc = store[r // 2, 0, b] - mu
+                dpc = store[r // 2, 1, a] - delta
+                tdc = store[r // 2, 1, b] - tdelta
+                ready[a, :] = (prob * (tsc * dpc + tdc)).astype(BF16)
+                ready[b, :] = (prob * dpc).astype(BF16)
+                ready[2 * TILE + c * SPAN:2 * TILE + (c + 1) * SPAN, :] = (prob * tsc).astype(BF16)
+
+        def add(r, ready):
+            here = pl.ds(pl.multiple_of((first_tile + r) * TILE, TILE), TILE)
+            hk_acc[here, :] += nn_dot(ready[0:TILE], q_rows[...])
+            hv_acc[here, :] += nn_dot(ready[2 * TILE:], g_rows[...])
+            keys = jnp.concatenate([k_t[:, here], tk_t[:, here]], axis=1)
+            hq_acc[...] += nn_dot(keys, ready[0:2 * TILE])
+
+        def grads_pair(u, carry):
+            weigh(2 * u + 1, odd, p_odd)
+            add(2 * u, p_even)
+            weigh(2 * u + 2, even, p_even)
+            add(2 * u + 1, p_odd)
             return carry
 
-        lax.fori_loop(first_tile, last_tile, grads_step, 0)
+        def grads_two():
+            weigh(tiles - 1, odd, p_odd)
+            add(tiles - 2, p_even)
+            add(tiles - 1, p_odd)
+
+        weigh(0, even, p_even)
+        lax.fori_loop(0, pairs, grads_pair, 0)
+        pl.when(one_left)(lambda: add(tiles - 1, p_even))
+        pl.when(jnp.logical_not(one_left))(grads_two)
         hq = (hq_acc[...] * SCALE).T.astype(BF16)
         for h in range(OWN_HEADS):
             hq_out[s, rows, h * HEAD:(h + 1) * HEAD] = hq[h * SPAN:(h + 1) * SPAN]
@@ -286,11 +351,10 @@
         first = pair[i]
         for half in range(2):
             block = first if half == 0 else BLOCKS - 1 - first
-            tile = block // (TILE // SPAN)
-            off = pl.multiple_of((block % (TILE // SPAN)) * SPAN, SPAN)
+            here = pl.ds(pl.multiple_of(block * SPAN, SPAN), SPAN)
             rows = pl.ds(half * SPAN, SPAN)
-            hk = hk_acc[tile, pl.ds(off, SPAN), :] * SCALE
-            hv = hv_acc[tile, pl.ds(off, SPAN), :]
+            hk = hk_acc[here, :] * SCALE
+            hv = hv_acc[here, :]
             carry = carry + fold_rows(kv[i, 2, rows, :].astype(F32) * hk)
             carry = carry + fold_rows(kv[i, 3, rows, :].astype(F32) * hv)
             z = i // HALF
@@ -316,11 +380,20 @@
         in_specs=[pl.BlockSpec(memory_space=pltpu.SMEM)] + [vmem] * 4,
         out_specs=(vmem,) * 3,
         scratch_shapes=[
-            pltpu.VMEM((TILES, 2 * TILE, HEAD), BF16),
-            pltpu.VMEM((TILES, 2 * TILE, HEAD), BF16),
-            pltpu.VMEM((TILES, HEAD, 2 * TILE), BF16),
-            pltpu.VMEM((TILES, TILE, HEAD), F32),
-            pltpu.VMEM((TILES, TILE, HEAD), F32),
+            pltpu.VMEM((2 * WINDOW, 2 * HEAD), BF16),
+            pltpu.VMEM((2 * WINDOW, HEAD), BF16),
+            pltpu.VMEM((HEAD, WINDOW), BF16),
+            pltpu.VMEM((HEAD, WINDOW), BF16),
+            pltpu.VMEM((2 * HEAD, ROWS), BF16),
+            pltpu.VMEM((HEAD, ROWS), BF16),
+            pltpu.VMEM((ROWS, HEAD), BF16),
+            pltpu.VMEM((ROWS, HEAD), BF16),
+            pltpu.VMEM(((TILES + 1) // 2, 2, 2 * TILE, ROWS), F32),
+            pltpu.VMEM(((TILES + 1) // 2, 2, 2 * TILE, ROWS), F32),
+            pltpu.VMEM((3 * TILE, ROWS), BF16),
+            pltpu.VMEM((3 * TILE, ROWS), BF16),
+            pltpu.VMEM((WINDOW, HEAD), F32),
+            pltpu.VMEM((WINDOW, HEAD), F32),
             pltpu.VMEM((HEAD, ROWS), F32),
         ],
         compiler_params=pltpu.CompilerParams(vmem_limit_bytes=50 << 20),

time: 178 us -> 132 us (0.74); the launches traced: 178 us -> 129 us
  Pallas kernels: 170 us -> 121 us
    pallas_call x1, Pallas kernels: 88 us -> 50 us  [hvp(): pl.pallas_call(hvp_kernel, out_shape=(jax.ShapeDtypeStruct((HALF, TOK, OW...]
    pallas_call x1, Pallas kernels: 43.1 us -> 32.7 us  [collect(): pl.pallas_call(collect_kernel, out_shape=(jax.ShapeDtypeStruct((TOK, QUER...]
where the time goes in v2:
time: 132 us; the launch traced here: 129 us
  Pallas kernels  121 us (92%)
  local copies, waits for them, and re-layouts  6.44 us (5%)
    pallas_call x1, Pallas kernels, hvp(): pl.pallas_call(hvp_kernel, out_shape=(jax.ShapeDtypeStruct((HALF, TOK, OW...  50 us
    pallas_call x1, Pallas kernels, spread(): pl.pallas_call(spread_kernel, out_shape=(jax.ShapeDtypeStruct((HALF, TOK,...  38.6 us
    pallas_call x1, Pallas kernels, collect(): pl.pallas_call(collect_kernel, out_shape=(jax.ShapeDtypeStruct((TOK, QUER...  32.7 us
    unnamed x10, local copies, waits for them, and re-layouts  5.39 us

profile of v2, /device:TPU:32, one launch (start us, length us, event | category | flops | bytes accessed | tf_op | source)
XLA Modules:
  0.0 129.2 jit_solution(11930968282222528031)
XLA Ops:
  0.6 1.2 copy.9
  1.8 0.2 copy.11
  2.0 1.2 copy.10
  3.1 0.0 copy-start.1
  3.1 0.0 copy-start.2
  3.1 0.2 copy.12
  3.3 0.8 maximum_bitcast_fusion.kv
  4.2 38.6 %spread.1 = (bf16[8,128,512]{2,1,0:T(8,128)(2,1)}, bf16[8,128,512]{2,1,0:T(8,128)(2,1)}, bf16[16,4,128,128]{3,2,1,0:T(8,128)(2,1)}) custom-call(bf16[128,4096]{1,0:T(8,128)(2,1)} %bitcast.14, bf16[128,4096]{1,0:T(8,128)(2,1)} %bitcast.15, bf16[4,4,128,128]{3,2,1,0:T(8,128)(2,1)} %maximum_bitcast_fusion.kv), custom_call_target="tpu_custom_call" | custom-call | tf_op jit(solution)/shard_map/spread/pallas_call | solution.py:126
  42.7 0.0 copy-done.1
  42.7 0.0 copy-done.2
  42.8 0.0 copy-start
  42.8 1.2 copy-done
  44.0 50.0 %hvp.1 = (bf16[8,128,512]{2,1,0:T(8,128)(2,1)S(1)}, bf16[2,2,4,2,128,128]{5,4,3,2,1,0:T(8,128)(2,1)S(1)}, f32[8,128]{1,0:T(8,128)S(1)}) custom-call(s32[16]{0:T(128)S(1)} %copy-done.2, s32[16,128]{1,0:T(8,128)S(1)} %bitcast.13, bf16[8,128,512]{2,1,0:T(8,128)(2,1)S(1)} %copy-done, bf16[8,128,512]{2,1,0:T(8,128)(2,1)} %get-tuple-element.13.g, ...), custom_call_target="tpu_custom_call" | custom-call | tf_op jit(solution)/shard_map/hvp/pallas_call | solution.py:373
  94.0 32.7 %collect.1 = (bf16[128,4096]{1,0:T(8,128)(2,1)S(1)}, bf16[4,2,128,128]{3,2,1,0:T(8,128)(2,1)S(1)}, f32[8,128]{1,0:T(8,128)S(1)}) custom-call(bf16[8,128,512]{2,1,0:T(8,128)(2,1)S(1)} %get-tuple-element.15.hq, bf16[2,2,4,2,128,128]{5,4,3,2,1,0:T(8,128)(2,1)S(1)} %get-tuple-element.16.hkv, f32[8,128]{1,0:T(8,128)S(1)} %get-tuple-element.17.curv), custom_call_target="tpu_custom_call" | custom-call | tf_op jit(solution)/shard_map/collect/pallas_call | solution.py:491
  126.7 0.5 slice.3
  127.2 0.2 copy.13
  127.4 0.9 copy.14
  128.3 1.0 copy.16
Async XLA Ops:
  3.1 39.6 %copy-start.1 = (s32[1,2048]{1,0:T(1,128)S(1)}, s32[1,2048]{1,0:T(1,128)}, u32[]{:S(2)}) copy-start(s32[1,2048]{1,0:T(1,128)} %param.10) | copy-start | bytes 24580
  3.1 39.6 %copy-start.2 = (s32[16]{0:T(128)S(1)}, s32[16]{0:T(128)}, u32[]{:S(2)}) copy-start(s32[16]{0:T(128)} %pair.1) | copy-start | bytes 196
  42.8 1.2 copy-start
